TPU v7x, 256 devices: a whole 4x4x8 slice. The times are simulated.
256 devices in a mesh: mp: 4 (over y), nodes: 64 (over z, x, core).
Axes of the slice: x: 4, y: 4, z: 8, core: 2. Of those that a mesh axis runs over, the one named last changes fastest.
Arguments:
- grid_latent: float32 [131072, 512], P('nodes'), may hold values from -6 to 6
- mesh_latent: float32 [8192, 512], P('nodes'), may hold values from -250 to 250
- enc_grid_w: float32 [512, 512], P(None, 'mp'), may hold values from -0.25 to 0.25
- enc_mesh_w: float32 [512, 512], P(None, 'mp'), may hold values from -0.25 to 0.25
- enc_out_w: float32 [512, 512], P('mp'), may hold values from -0.25 to 0.25
- block_gain: float32 [512], replicated, may hold values from 0.5 to 1.5
- query_w: float32 [512, 512], P(None, 'mp'), may hold values from -1 to 1
- key_w: float32 [512, 512], P(None, 'mp'), may hold values from -1 to 1
- value_w: float32 [512, 512], P(None, 'mp'), may hold values from -0.25 to 0.25
- out_w: float32 [512, 512], P('mp'), may hold values from -0.25 to 0.25
- up_w: float32 [512, 2048], P(None, 'mp'), may hold values from -0.25 to 0.25
- down_w: float32 [2048, 512], P('mp'), may hold values from -0.125 to 0.125
- dec_gain: float32 [512], replicated, may hold values from 0.5 to 1.5
- dec_grid_w: float32 [512, 512], P(None, 'mp'), may hold values from -0.25 to 0.25
- dec_mesh_w: float32 [512, 512], P(None, 'mp'), may hold values from -0.25 to 0.25
- dec_out_w: float32 [512, 512], P('mp'), may hold values from -0.25 to 0.25
- neighbor_blocks: int32 [64, 16], replicated, may hold values from 0 to 63, as said below
- enc_tiles: int32 [2048, 2], P('nodes'), may hold values from -1 to 1023, as said below
- enc_edges: int32 [2048, 2, 128], P('nodes'), may hold values from 0 to 127
- dec_tiles: int32 [3072, 2], P('nodes'), may hold values from 0 to 1023, as said below
- dec_edges: int32 [3072, 2, 128], P('nodes'), may hold values from 0 to 127
Outputs:
- grid_out: float32 [131072, 512], P('nodes', 'mp')
Inputs may be any that keep to these rules, and one draw needn't show every extreme that they name: `neighbor_blocks`: rows i * 1 to (i + 1) - 1 are the query blocks of index i of nodes; among all entries of those rows, the blocks of any one index j of nodes (ids j * 1 to (j + 1) - 1) are named at most 1 times, and for every i some j is named exactly 1 times. Entries may repeat. `enc_tiles`: tile slots i * 32 to (i + 1) * 32 - 1 belong to index i of nodes; a live tile names a grid block and a mesh block both of index i; an unused slot holds -1 in both columns; on each index the live slots come first, their number differs between indices, and some index has all 32 slots live. `dec_tiles`: tiles i * 48 to (i + 1) * 48 - 1 belong to index i of nodes; each names a grid block of index i and a mesh block of index i - 1, i or i + 1 of nodes (counted around the axis).
All inputs are finite; a program needn't handle non-finite values.
Results may differ from a plain program's by a relative error of at most 0.000098.
Values sent between devices are 32-bit elements; how exact they have to be, the bound alone decides.
A program may use at most 128 MiB of HBM per device.

v0:
```python
import math
import jax
import jax.numpy as jnp
from jax import lax
from jax.sharding import PartitionSpec as P

HEAD_DIM = 128
NODE_BLOCK = 128
FULL_PRECISION = lax.Precision.HIGHEST


def copy_for_each(shard, axis):
    devices = lax.axis_size(axis)
    return lax.all_to_all(
        jnp.broadcast_to(shard[None], (devices, *shard.shape)), axis, 0, 0, tiled=True
    )


def taken_together(shard, axis):
    everything = copy_for_each(shard, axis)
    return jnp.sum(everything, axis=0)


def padded(shard, sides, width):
    for axis, dim in sides:
        devices, length = (lax.axis_size(axis), shard.shape[dim])
        up = [(i, (i + 1) % devices) for i in range(devices)]
        down = [(j, i) for i, j in up]
        last = lax.slice_in_dim(shard, length - width, length, axis=dim)
        initial = lax.slice_in_dim(shard, 0, width, axis=dim)
        before = lax.ppermute(last, axis, up)
        after = lax.ppermute(initial, axis, down)
        shard = jnp.concatenate([before, shard, after], axis=dim)
    return shard


def product(matrix, weight):
    return jnp.dot(matrix, weight, precision=FULL_PRECISION, preferred_element_type=jnp.float32)


def layer_norm(inputs, scales):
    centre = jnp.mean(inputs, axis=-1, keepdims=True)
    shifted = inputs - centre
    spread = jnp.mean(shifted * shifted, axis=-1, keepdims=True)
    return shifted * lax.rsqrt(spread + 1e-05) * scales


def edge_pass(
    source_side, target_side, source_block, target_block, edge_ids, tile_live, target_blocks
):
    source = source_block[:, None] * NODE_BLOCK + edge_ids[:, 0, :]
    target = target_block[:, None] * NODE_BLOCK + edge_ids[:, 1, :]
    message = jax.nn.silu(source_side[source] + target_side[target]) * tile_live[:, None, None]
    within = (edge_ids[:, 1, :][:, None, :] == jnp.arange(NODE_BLOCK)[None, :, None]).astype(
        jnp.float32
    )
    tile_sums = jnp.einsum("tne,teh->tnh", within, message, precision=FULL_PRECISION)
    placing = (target_block[None, :] == jnp.arange(target_blocks)[:, None]).astype(jnp.float32)
    summed = jnp.einsum("bt,tnh->bnh", placing, tile_sums, precision=FULL_PRECISION)
    return summed.reshape(target_blocks * NODE_BLOCK, -1)


def per_device(
    grid_latent,
    mesh_latent,
    enc_grid_w,
    enc_mesh_w,
    enc_out_w,
    block_gain,
    query_w,
    key_w,
    value_w,
    out_w,
    up_w,
    down_w,
    dec_gain,
    dec_grid_w,
    dec_mesh_w,
    dec_out_w,
    neighbor_blocks,
    enc_tiles,
    enc_edges,
    dec_tiles,
    dec_edges,
):
    me_node = lax.axis_index("nodes")
    nodes_count = lax.axis_size("nodes")
    grid_rows = grid_latent.shape[0]
    node_rows = mesh_latent.shape[0]
    grid_blocks = grid_rows // NODE_BLOCK
    node_blocks = node_rows // NODE_BLOCK
    grid_enc = product(grid_latent, enc_grid_w)
    mesh_enc = product(mesh_latent, enc_mesh_w)
    tile_live = enc_tiles[:, 0] >= 0
    source_block = jnp.where(tile_live, enc_tiles[:, 0] - me_node * grid_blocks, 0)
    target_block = jnp.where(tile_live, enc_tiles[:, 1] - me_node * node_blocks, 0)
    enc_agg = edge_pass(
        grid_enc,
        mesh_enc,
        source_block,
        target_block,
        enc_edges,
        tile_live.astype(jnp.float32),
        node_blocks,
    )
    enc_total = taken_together(product(enc_agg, enc_out_w), "mp")
    mesh_one = mesh_latent + enc_total
    normed = layer_norm(mesh_one, block_gain)
    queries = product(normed, query_w)
    key_rows = product(normed, key_w)
    value_rows = product(normed, value_w)
    head_cols = queries.shape[1]
    heads_here = head_cols // HEAD_DIM
    key_values = jnp.concatenate([key_rows, value_rows], axis=1)
    query_blocks = queries.reshape(node_blocks, NODE_BLOCK, heads_here, HEAD_DIM)
    own_lists = lax.dynamic_slice_in_dim(neighbor_blocks, me_node * node_blocks, node_blocks, 0)
    key_piece = lax.all_gather(key_values, "nodes", axis=0, tiled=True)
    running_max = jnp.full((node_blocks, heads_here, NODE_BLOCK), -1e30, jnp.float32)
    row_count = key_piece.shape[0]
    piece_block = jnp.arange(row_count) // NODE_BLOCK
    repeats = jnp.sum(
        (own_lists[:, :, None] == piece_block[None, None, :]).astype(jnp.float32), axis=1
    )
    near_keys = key_piece[:, :head_cols].reshape(row_count, heads_here, HEAD_DIM)
    near_values = key_piece[:, head_cols:].reshape(row_count, heads_here, HEAD_DIM)
    scores = jnp.einsum(
        "bqhd,khd->bhqk", query_blocks, near_keys, precision=FULL_PRECISION
    ) / math.sqrt(HEAD_DIM)
    scores = jnp.where((repeats > 0)[:, None, None, :], scores, -1e30)
    new_max = jnp.maximum(running_max, jnp.max(scores, axis=-1))
    weights = jnp.exp(scores - new_max[..., None]) * repeats[:, None, None, :]
    running_sum = jnp.sum(weights, axis=-1)
    running_out = jnp.einsum("bhqk,khd->bhqd", weights, near_values, precision=FULL_PRECISION)
    running_max, running_sum, running_out = (new_max, running_sum, running_out)
    attended = (
        (running_out / running_sum[..., None]).transpose(0, 2, 1, 3).reshape(node_rows, head_cols)
    )
    hidden = jax.nn.silu(product(normed, up_w))
    block_total = taken_together(product(attended, out_w) + product(hidden, down_w), "mp")
    mesh_two = mesh_one + block_total
    mesh_normed = layer_norm(mesh_two, dec_gain)
    all_blocks = node_blocks * nodes_count
    dec_source = (dec_tiles[:, 0] - (me_node - 1) * node_blocks) % all_blocks
    dec_target = dec_tiles[:, 1] - me_node * grid_blocks
    mesh_dec = product(mesh_normed, dec_mesh_w)
    grid_dec = product(grid_latent, dec_grid_w)
    beside_all = padded(mesh_dec, (("nodes", 0),), node_rows)
    every_tile = jnp.ones((dec_tiles.shape[0],), jnp.float32)
    dec_agg = edge_pass(
        beside_all, grid_dec, dec_source, dec_target, dec_edges, every_tile, grid_blocks
    )
    decoded = lax.psum_scatter(product(dec_agg, dec_out_w), "mp", scatter_dimension=1, tiled=True)
    share_cols = decoded.shape[1]
    grid_share = lax.dynamic_slice_in_dim(
        grid_latent, lax.axis_index("mp") * share_cols, share_cols, 1
    )
    return grid_share + decoded


def solution(mesh):
    in_specs = (
        P("nodes", None),
        P("nodes", None),
        P(None, "mp"),
        P(None, "mp"),
        P("mp", None),
        P(),
        P(None, "mp"),
        P(None, "mp"),
        P(None, "mp"),
        P("mp", None),
        P(None, "mp"),
        P("mp", None),
        P(),
        P(None, "mp"),
        P(None, "mp"),
        P("mp", None),
        P(),
        P("nodes", None),
        P("nodes", None, None),
        P("nodes", None),
        P("nodes", None, None),
    )
    out_specs = P("nodes", "mp")
    return jax.shard_map(
        per_device, mesh=mesh, in_specs=in_specs, out_specs=out_specs, check_vma=False
    )
```

profile of v0, /device:TPU:1, one launch (start us, length us, event | category | flops | bytes accessed | tf_op | source)
XLA Modules:
  0.0 320.2 jit_solution(5665436345619726725)
XLA Ops:
  8.1 0.9 fusion.91
  8.9 5.2 %fusion.94 = f32[2048,128]{1,0:T(8,128)S(1)} fusion(f32[2048,512]{1,0:T(8,128)} %param.21, f32[512,128]{1,0:T(8,128)} %param.23), kind=kOutput, calls=%fused_computation.123 | convolution fusion | flops 1610612736 | bytes 5505024 | tf_op jit(solution)/shard_map/dot_general | solution.py:38
  14.3 14.1 %gather_fusion = f32[4096,128]{1,0:T(8,128)} fusion(f32[2048,128]{1,0:T(8,128)S(1)} %fusion.94, s32[4096]{0:T(1024)S(1)} %get-tuple-element.20), kind=kCustom, calls=%fused_computation | custom fusion | bytes 4210688 | tf_op jit(solution)/shard_map/gather | solution.py:53
  28.8 14.1 %gather_fusion.1 = f32[4096,128]{1,0:T(8,128)} fusion(f32[128,128]{1,0:T(8,128)S(1)} %fusion.95, s32[4096]{0:T(1024)S(1)} %get-tuple-element.21), kind=kCustom, calls=%fused_computation.1 | custom fusion | bytes 4210688 | tf_op jit(solution)/shard_map/gather | solution.py:53
  42.9 1.8 add.221
  44.7 1.9 fusion.19
  46.6 2.0 fusion.15
  49.1 19.0 %all_to_all.10 = f32[4,128,512]{2,1,0:T(8,128)S(1)} all-to-all(f32[4,128,512]{2,1,0:T(8,128)S(1)} %broadcast_in_dim.17), channel_id=1, replica_groups=mesh['mp'=4,'nodes'=64] {'mp'}, dimensions={0} | all-to-all | bytes 2097152 | tf_op jit(solution)/shard_map/all_to_all | solution.py:14
  68.2 1.1 fusion.89
  69.6 1.6 fusion.87
  71.2 1.6 fusion.86
  73.9 1.4 fusion.85
  76.8 84.9 %all-gather.2.cloned.1.call-done = f32[8192,256]{0,1:T(8,128)} async-done(((f32[128,256]{0,1:T(8,128)}), f32[8192,256]{0,1:T(8,128)}) %all-gather.2.cloned.1.call-update) | async-done | bytes 8388624 | tf_op jit(solution)/shard_map/all_gather | solution.py:117
  161.6 10.2 %fusion.92 = (f32[128]{0:T(128)S(1)}, f32[1,8192,1,128]{3,1,2,0:T(8,128)S(1)}) fusion(f32[128,128]{1,0:T(8,128)S(1)} %fusion.85, f32[8192,256]{0,1:T(8,128)} %all-gather.2.cloned.1.call-done, pred[8192]{0:T(1024)(128)(4,1)S(1)} %broadcast_compare_fusion), kind=kOutput, calls=%fused_computation.121 | convolution fusion | flops 1613758336 | bytes 8462848 | tf_op jit(solution)/shard_map/bqhd,khd->bhqk/dot_general | solution.py:126
  171.8 3.5 %fusion.6 = f32[128]{0:T(128)S(1)} fusion(f32[1,8192,1,128]{3,1,2,0:T(8,128)S(1)} %get-tuple-element.19, f32[8192]{0:T(1024)S(1)} %convert_reduce_fusion, f32[128]{0:T(128)S(1)} %broadcast_maximum_fusion), kind=kLoop, calls=%fused_computation.12 | loop fusion | flops 3145600 | bytes 4228096 | tf_op jit(solution)/shard_map/reduce_sum | solution.py:132
  175.3 5.0 %fusion.38 = f32[128,128]{0,1:T(8,128)S(1)} fusion(f32[1,8192,1,128]{3,1,2,0:T(8,128)S(1)} %get-tuple-element.19, f32[8192]{0:T(1024)S(1)} %convert_reduce_fusion, f32[128]{0:T(128)S(1)} %broadcast_maximum_fusion, f32[8192,256]{0,1:T(8,128)S(1)} %copy-done.1, f32[128]{0:T(128)S(1)} %fusion.6), kind=kOutput, calls=%fused_computation.39 | convolution fusion | flops 1612726272 | bytes 8487936 | tf_op jit(solution)/shard_map/bhqk,khd->bhqd/dot_general | solution.py:133
  180.8 1.1 broadcast_in_dim.21
  181.9 4.0 %all-to-all-start.1 = ((f32[4,128,512]{2,1,0:T(8,128)}), f32[4,128,512]{2,1,0:T(8,128)S(1)}, u32[]{:S(2)}, u32[]{:S(2)}) async-start(f32[4,128,512]{2,1,0:T(8,128)} %broadcast_in_dim.21), calls=%async_computation.1 | async-start | bytes 2097152 | tf_op jit(solution)/shard_map/all_to_all | solution.py:14
  186.0 5.2 %fusion.97 = f32[2048,128]{1,0:T(8,128)S(1)} fusion(f32[2048,512]{1,0:T(8,128)} %param.21, f32[512,128]{1,0:T(8,128)} %param.34), kind=kOutput, calls=%fused_computation.126 | convolution fusion | flops 1610612736 | bytes 5505024 | tf_op jit(solution)/shard_map/dot_general | solution.py:38
  191.2 9.3 %all-to-all-done.1 = f32[4,128,512]{2,1,0:T(8,128)S(1)} async-done(((f32[4,128,512]{2,1,0:T(8,128)}), f32[4,128,512]{2,1,0:T(8,128)S(1)}, u32[]{:S(2)}, u32[]{:S(2)}) %all-to-all-start.1) | async-done | bytes 1048608 | tf_op jit(solution)/shard_map/all_to_all | solution.py:14
  200.6 0.8 reduce_sum.77
  201.4 1.1 fusion.88
  202.6 1.4 fusion.46
  204.0 3.1 collective-permute-start
  207.2 20.9 %gather_fusion.3 = f32[6144,128]{1,0:T(8,128)} fusion(f32[2048,128]{1,0:T(8,128)S(1)} %fusion.97, s32[6144]{0:T(1024)S(1)} %get-tuple-element.23), kind=kCustom, calls=%fused_computation.3 | custom fusion | bytes 6316032 | tf_op jit(solution)/shard_map/gather | solution.py:53
  228.1 20.9 %gather_fusion.2 = f32[6144,128]{1,0:T(8,128)} fusion(f32[384,128]{1,0:T(8,128)S(1)} %pad_maximum_fusion, s32[6144]{0:T(1024)S(1)} %get-tuple-element.22), kind=kCustom, calls=%fused_computation.2 | custom fusion | bytes 6316032 | tf_op jit(solution)/shard_map/gather | solution.py:53
  249.1 3.2 add.222
  252.2 2.9 fusion.9
  255.2 2.9 fusion.7
  258.5 4.9 %fusion.98 = f32[2048,512]{1,0:T(8,128)} fusion(f32[2048,128]{1,0:T(8,128)S(1)} %bitcast.97, f32[128,512]{1,0:T(8,128)S(1)} %copy-done.8), kind=kOutput, calls=%fused_computation.127 | convolution fusion | flops 1610612736 | bytes 5505024 | tf_op jit(solution)/shard_map/dot_general | solution.py:38
  263.4 47.3 %reduce-scatter.2.cloned.1.call-done = f32[2048,128]{1,0:T(8,128)} async-done(((f32[2048,512]{1,0:T(8,128)}), f32[2048,128]{1,0:T(8,128)}) %reduce-scatter.2.cloned.1.call-update) | async-done | bytes 1048592 | tf_op jit(solution)/shard_map/reduce_scatter | solution.py:152
  310.7 2.6 dynamic-slice_add_fusion
  (64 shorter events, 6.5 us)
Async XLA Ops:
  6.5 68.7 %copy-start = (f32[512,512]{1,0:T(8,128)S(1)}, f32[512,512]{1,0:T(8,128)}, u32[]{:S(2)}) copy-start(f32[512,512]{1,0:T(8,128)} %param.31) | copy-start | bytes 3145732
  6.5 155.1 %all-gather.2.cloned.1.call-start = ((), (), s32[]{:S(2)}) async-start(), calls=%async_computation.3 | async-start | bytes 8519680 | tf_op jit(solution)/shard_map/all_gather | solution.py:117
  14.2 14.1 %copy-start.4 = (f32[128,512]{1,0:T(8,128)S(1)}, f32[128,512]{1,0:T(8,128)}, u32[]{:S(2)}) copy-start(f32[128,512]{1,0:T(8,128)} %param.22) | copy-start | bytes 786436
  14.3 14.1 %copy-start.5 = (f32[512,128]{1,0:T(8,128)S(1)}, f32[512,128]{1,0:T(8,128)}, u32[]{:S(2)}) copy-start(f32[512,128]{1,0:T(8,128)} %param.24) | copy-start | bytes 786436
  28.8 14.1 %copy-start.2 = (f32[4096,128]{1,0:T(8,128)S(1)}, f32[4096,128]{1,0:T(8,128)}, u32[]{:S(2)}) copy-start(f32[4096,128]{1,0:T(8,128)} %gather_fusion) | copy-start | bytes 6291460
  44.7 1.9 copy-start.12
  44.7 3.9 %copy-start.6 = (f32[128,512]{1,0:T(8,128)S(1)}, f32[128,512]{1,0:T(8,128)}, u32[]{:S(2)}) copy-start(f32[128,512]{1,0:T(8,128)} %param.25) | copy-start | bytes 786436
  48.6 21.0 %copy-start.10 = (f32[512]{0:T(512)S(1)}, f32[512]{0:T(512)}, u32[]{:S(2)}) copy-start(f32[512]{0:T(512)} %param.26) | copy-start | bytes 6148
  49.1 24.4 %copy-start.11 = (s32[64,16]{0,1:T(8,128)S(1)}, s32[64,16]{0,1:T(8,128)}, u32[]{:S(2)}) copy-start(s32[64,16]{0,1:T(8,128)} %param.37) | copy-start | bytes 12292
  68.1 7.9 %copy-start.3 = (f32[512,512]{1,0:T(8,128)S(1)}, f32[512,512]{1,0:T(8,128)}, u32[]{:S(2)}) copy-start(f32[512,512]{1,0:T(8,128)} %param.32) | copy-start | bytes 3145732
  161.6 13.7 %copy-start.1 = (f32[8192,256]{0,1:T(8,128)S(1)}, f32[8192,256]{0,1:T(8,128)}, u32[]{:S(2)}) copy-start(f32[8192,256]{0,1:T(8,128)} %all-gather.2.cloned.1.call-done) | copy-start | bytes 25165828
  175.3 5.0 %copy-start.7 = (f32[128,512]{1,0:T(8,128)S(1)}, f32[128,512]{1,0:T(8,128)}, u32[]{:S(2)}) copy-start(f32[128,512]{1,0:T(8,128)} %param.30) | copy-start | bytes 786436
  180.3 5.6 %copy-start.14 = (s32[48,2]{0,1:T(2,128)S(1)}, s32[48,2]{0,1:T(2,128)}, u32[]{:S(2)}) copy-start(s32[48,2]{0,1:T(2,128)} %param.40) | copy-start | bytes 1156
  180.4 5.6 %copy-start.9 = (s32[48,2,128]{2,1,0:T(2,128)S(1)}, s32[48,2,128]{2,1,0:T(2,128)}, u32[]{:S(2)}) copy-start(s32[48,2,128]{2,1,0:T(2,128)} %param.41) | copy-start | bytes 147460
  181.9 18.7 %all-to-all-start.1 = ((f32[4,128,512]{2,1,0:T(8,128)}), f32[4,128,512]{2,1,0:T(8,128)S(1)}, u32[]{:S(2)}, u32[]{:S(2)}) async-start(f32[4,128,512]{2,1,0:T(8,128)} %broadcast_in_dim.21), calls=%async_computation.1 | async-start | bytes 2097152 | tf_op jit(solution)/shard_map/all_to_all | solution.py:14
  185.9 124.8 %reduce-scatter.2.cloned.1.call-start = ((), (), s32[]{:S(2)}) async-start(), calls=%async_computation.4 | async-start | bytes 5242880 | tf_op jit(solution)/shard_map/reduce_scatter | solution.py:152
  186.0 16.6 %copy-start.13 = (f32[512]{0:T(512)S(1)}, f32[512]{0:T(512)}, u32[]{:S(2)}) copy-start(f32[512]{0:T(512)} %param.33) | copy-start | bytes 6148
  204.0 24.1 %collective-permute-start = (f32[128,128]{1,0:T(8,128)S(1)}, f32[128,128]{1,0:T(8,128)S(1)}, u32[]{:S(2)}, u32[]{:S(2)}) collective-permute-start(f32[128,128]{1,0:T(8,128)S(1)} %fusion.46), channel_id=1, source_target_pairs={{0,1},{1,2},{2,3},{3,4},{4,5},{5,6},{6,7},{7,8},{8,9},{9,10},{10,1... | collective-permute-start | bytes 196616 | tf_op jit(solution)/shard_map/ppermute | solution.py:31
  207.1 21.0 %collective-permute-start.1 = (f32[128,128]{1,0:T(8,128)S(1)}, f32[128,128]{1,0:T(8,128)S(1)}, u32[]{:S(2)}, u32[]{:S(2)}) collective-permute-start(f32[128,128]{1,0:T(8,128)S(1)} %fusion.46), channel_id=1, source_target_pairs={{1,0},{2,1},{3,2},{4,3},{5,4},{6,5},{7,6},{8,7},{9,8},{10,9},{11,1... | collective-permute-start | bytes 196616 | tf_op jit(solution)/shard_map/ppermute | solution.py:32
  255.2 3.3 %copy-start.8 = (f32[128,512]{1,0:T(8,128)S(1)}, f32[128,512]{1,0:T(8,128)}, u32[]{:S(2)}) copy-start(f32[128,512]{1,0:T(8,128)} %param.36) | copy-start | bytes 786436
Sparse Core Ops, SparseCore 0:
  73.6 87.9 all-gather.1
  263.6 47.1 reduce-scatter.1
where the time goes:
time: 321 us; the launch traced here: 320 us
  waiting for transfers between devices  142 us (44%)
  local copies, waits for them, and re-layouts  72.8 us (23%)
  matrix products  48.9 us (15%)
  blocking collectives  19 us (6%)
  other arithmetic  17.1 us (5%)
  between operations  13.8 us (4%)
  starting transfers between devices  7.08 us (2%)
    all_gather x1, waiting for transfers between devices, per_device(): key_piece = lax.all_gather(key_values, 'nodes', axis=0, tiled=True)  84.9 us
    reduce_scatter x1, waiting for transfers between devices, per_device(): lax.psum_scatter(product(dec_agg, dec_out_w), 'mp', scatter_dimension=1,...  47.3 us
    gather x2, local copies, waits for them, and re-layouts, edge_pass(): source_side[source] + target_side[target]  35 us
    gather x2, local copies, waits for them, and re-layouts, edge_pass(): target_side[target]  35 us
    dot_general x12, matrix products, product(): jnp.dot(matrix, weight, precision=FULL_PRECISION, preferred_element_type=...  24 us
    all_to_all x1, blocking collectives, copy_for_each(): lax.all_to_all(jnp.broadcast_to(shard[None], (devices, *shard.shape)), ax...  19 us
    dot_general x1, matrix products, per_device(): jnp.einsum('bqhd,khd->bhqk', query_blocks, near_keys, precision=FULL_PREC...  10.2 us
    all_to_all x1, waiting for transfers between devices, copy_for_each(): lax.all_to_all(jnp.broadcast_to(shard[None], (devices, *shard.shape)), ax...  9.34 us
  transfers between devices with their start and end apart: 5, of which 3 were waited for; matrix products, arithmetic and copies ran while one was open for 9% of the time, Pallas kernels for 0%

commit v1 on v0

--- a/solution.py
+++ b/solution.py
@@ -7,6 +7,11 @@
 HEAD_DIM = 128
 NODE_BLOCK = 128
 FULL_PRECISION = lax.Precision.HIGHEST
+
+
+def gather_from_all(x, axis, dim):
+    copies = jnp.concatenate([x] * lax.axis_size(axis), axis=dim)
+    return lax.all_to_all(copies, axis, dim, dim, tiled=True)
 
 
 def copy_for_each(shard, axis):
@@ -114,7 +119,7 @@
     key_values = jnp.concatenate([key_rows, value_rows], axis=1)
     query_blocks = queries.reshape(node_blocks, NODE_BLOCK, heads_here, HEAD_DIM)
     own_lists = lax.dynamic_slice_in_dim(neighbor_blocks, me_node * node_blocks, node_blocks, 0)
-    key_piece = lax.all_gather(key_values, "nodes", axis=0, tiled=True)
+    key_piece = gather_from_all(key_values, "nodes", 0)
     running_max = jnp.full((node_blocks, heads_here, NODE_BLOCK), -1e30, jnp.float32)
     row_count = key_piece.shape[0]
     piece_block = jnp.arange(row_count) // NODE_BLOCK

time: 321 us -> 459 us (1.43); the launches traced: 320 us -> 450 us
  waiting for transfers between devices: 142 us -> 232 us
  starting transfers between devices: 7.08 us -> 37 us
  local copies, waits for them, and re-layouts: 72.8 us -> 86.6 us
    all_to_all x0 -> x1, waiting for transfers between devices: none -> 180 us  [gather_from_all(): return lax.all_to_all(copies, axis, dim, dim, tiled=True)]
    all_gather x1 -> x0, waiting for transfers between devices: 84.9 us -> none  [per_device(): key_piece = lax.all_gather(key_values, 'nodes', axis=0, tiled=True)]
    all_to_all x0 -> x1, starting transfers between devices: none -> 25.2 us  [gather_from_all(): return lax.all_to_all(copies, axis, dim, dim, tiled=True)]
    all_to_all x0 -> x2, local copies, waits for them, and re-layouts: none -> 13.3 us  [gather_from_all(): return lax.all_to_all(copies, axis, dim, dim, tiled=True)]
    ppermute x1, starting transfers between devices: 3.07 us -> 8.23 us  [padded(): before = lax.ppermute(last, axis, up)]
  transfers between devices with their start and end apart: 5 -> 5, of which waited for: 3 -> 3; matrix products, arithmetic and copies ran while one was open for 9% -> 6% of each run, Pallas kernels for 0% -> 0%
where the time goes in v1:
time: 459 us; the launch traced here: 450 us
  waiting for transfers between devices  232 us (51%)
  local copies, waits for them, and re-layouts  86.6 us (19%)
  matrix products  45.7 us (10%)
  starting transfers between devices  37 us (8%)
  blocking collectives  19 us (4%)
  between operations  14.8 us (3%)
  other arithmetic  14.6 us (3%)
    all_to_all x1, waiting for transfers between devices, gather_from_all(): return lax.all_to_all(copies, axis, dim, dim, tiled=True)  180 us
    reduce_scatter x1, waiting for transfers between devices, per_device(): lax.psum_scatter(product(dec_agg, dec_out_w), 'mp', scatter_dimension=1,...  46.9 us
    gather x2, local copies, waits for them, and re-layouts, edge_pass(): source_side[source] + target_side[target]  35.3 us
    gather x2, local copies, waits for them, and re-layouts, edge_pass(): target_side[target]  35.3 us
    all_to_all x1, starting transfers between devices, gather_from_all(): return lax.all_to_all(copies, axis, dim, dim, tiled=True)  25.2 us
    dot_general x12, matrix products, product(): jnp.dot(matrix, weight, precision=FULL_PRECISION, preferred_element_type=...  20.2 us
    all_to_all x1, blocking collectives, copy_for_each(): lax.all_to_all(jnp.broadcast_to(shard[None], (devices, *shard.shape)), ax...  19 us
    all_to_all x2, local copies, waits for them, and re-layouts, gather_from_all(): return lax.all_to_all(copies, axis, dim, dim, tiled=True)  13.3 us
  transfers between devices with their start and end apart: 5, of which 3 were waited for; matrix products, arithmetic and copies ran while one was open for 6% of the time, Pallas kernels for 0%

profile of v1, /device:TPU:1, one launch (start us, length us, event | category | flops | bytes accessed | tf_op | source)
XLA Modules:
  0.0 449.8 jit_solution(13438826603909842274)
XLA Ops:
  6.5 0.8 convert_bitcast_fusion
  7.3 0.8 multiply_bitcast_fusion.1
  8.1 0.9 fusion.91
  8.9 5.2 %fusion.94 = f32[2048,128]{1,0:T(8,128)S(1)} fusion(f32[2048,512]{1,0:T(8,128)} %param.21, f32[512,128]{1,0:T(8,128)} %param.23), kind=kOutput, calls=%fused_computation.188 | convolution fusion | flops 1610612736 | bytes 5505024 | tf_op jit(solution)/shard_map/dot_general | solution.py:43
  14.3 14.2 %gather_fusion = f32[4096,128]{1,0:T(8,128)} fusion(f32[2048,128]{1,0:T(8,128)S(1)} %fusion.94, s32[4096]{0:T(1024)S(1)} %get-tuple-element.22), kind=kCustom, calls=%fused_computation | custom fusion | bytes 4210688 | tf_op jit(solution)/shard_map/gather | solution.py:58
  28.9 14.2 %gather_fusion.1 = f32[4096,128]{1,0:T(8,128)} fusion(f32[128,128]{1,0:T(8,128)S(1)} %fusion.95, s32[4096]{0:T(1024)S(1)} %get-tuple-element.23), kind=kCustom, calls=%fused_computation.1 | custom fusion | bytes 4210688 | tf_op jit(solution)/shard_map/gather | solution.py:58
  43.1 1.8 add.221
  45.0 1.9 fusion.19
  46.9 2.0 fusion.15
  49.3 19.0 %all_to_all.22 = f32[4,128,512]{2,1,0:T(8,128)S(1)} all-to-all(f32[4,128,512]{2,1,0:T(8,128)S(1)} %broadcast_in_dim.17), channel_id=1, replica_groups=mesh['mp'=4,'nodes'=64] {'mp'}, dimensions={0} | all-to-all | bytes 2097152 | tf_op jit(solution)/shard_map/all_to_all | solution.py:19
  71.3 4.3 copy_bitcast_fusion
  75.7 25.2 %all-to-all-start.1 = ((f32[64,128,256]{1,2,0:T(8,128)}), f32[64,128,256]{1,2,0:T(8,128)}, u32[]{:S(2)}, u32[]{:S(2)}) async-start(f32[64,128,256]{1,2,0:T(8,128)} %copy_bitcast_fusion), calls=%async_computation.1 | async-start | bytes 16777216 | tf_op jit(solution)/shard_map/all_to_all | solution.py:14
  101.8 0.7 fusion.84
  102.5 0.8 fusion.49
  103.3 179.9 %all-to-all-done.1 = f32[64,128,256]{1,2,0:T(8,128)} async-done(((f32[64,128,256]{1,2,0:T(8,128)}), f32[64,128,256]{1,2,0:T(8,128)}, u32[]{:S(2)}, u32[]{:S(2)}) %all-to-all-start.1) | async-done | bytes 8388640 | tf_op jit(solution)/shard_map/all_to_all | solution.py:14
  283.2 9.0 %copy.41 = f32[64,128,256]{2,1,0:T(8,128)} copy(f32[64,128,256]{1,2,0:T(8,128)} %all-to-all-done.1) | data formatting | bytes 16777216 | tf_op jit(solution)/shard_map/all_to_all | solution.py:14
  292.2 7.8 %fusion.92 = (f32[128]{0:T(128)S(1)}, f32[1,8192,1,128]{3,1,2,0:T(8,128)S(1)}) fusion(f32[128,128]{1,0:T(8,128)S(1)} %fusion.85, f32[8192,256]{1,0:T(8,128)} %bitcast.103, pred[8192]{0:T(1024)(128)(4,1)S(1)} %broadcast_compare_fusion), kind=kOutput, calls=%fused_computation.186 | convolution fusion | flops 1613758336 | bytes 8462848 | tf_op jit(solution)/shard_map/bqhd,khd->bhqk/dot_general | solution.py:131
  300.0 3.5 fusion.6
  303.5 8.0 %fusion.38 = f32[128,128]{0,1:T(8,128)S(1)} fusion(f32[1,8192,1,128]{3,1,2,0:T(8,128)S(1)} %get-tuple-element.19, f32[8192]{0:T(1024)S(1)} %convert_reduce_fusion, f32[128]{0:T(128)S(1)} %broadcast_maximum_fusion, f32[8192,256]{1,0:T(8,128)S(1)} %bitcast.104, f32[128]{0:T(128)S(1)} %fusion.6), kind=kOutput, calls=%fused_computation.40 | convolution fusion | flops 1612726272 | bytes 8487936 | tf_op jit(solution)/shard_map/bhqk,khd->bhqd/dot_general | solution.py:138
  312.0 1.1 broadcast_in_dim.21
  313.1 3.5 all-to-all-start.2
  316.8 5.2 %fusion.97 = f32[2048,128]{1,0:T(8,128)S(1)} fusion(f32[2048,512]{1,0:T(8,128)} %param.21, f32[512,128]{1,0:T(8,128)S(1)} %copy-done.13), kind=kOutput, calls=%fused_computation.191 | convolution fusion | flops 1610612736 | bytes 5505024 | tf_op jit(solution)/shard_map/dot_general | solution.py:43
  322.0 5.3 %all-to-all-done.2 = f32[4,128,512]{2,1,0:T(8,128)S(1)} async-done(((f32[4,128,512]{2,1,0:T(8,128)}), f32[4,128,512]{2,1,0:T(8,128)S(1)}, u32[]{:S(2)}, u32[]{:S(2)}) %all-to-all-start.2) | async-done | bytes 1048608 | tf_op jit(solution)/shard_map/all_to_all | solution.py:19
  328.2 8.2 %collective-permute-start = (f32[128,128]{1,0:T(8,128)S(1)}, f32[128,128]{1,0:T(8,128)S(1)}, u32[]{:S(2)}, u32[]{:S(2)}) collective-permute-start(f32[128,128]{1,0:T(8,128)S(1)} %fusion.46), channel_id=1, source_target_pairs={{0,1},{1,2},{2,3},{3,4},{4,5},{5,6},{6,7},{7,8},{8,9},{9,10},{10,1... | collective-permute-start | bytes 196616 | tf_op jit(solution)/shard_map/ppermute | solution.py:36
  336.5 21.1 %gather_fusion.3 = f32[6144,128]{1,0:T(8,128)} fusion(f32[2048,128]{1,0:T(8,128)S(1)} %fusion.97, s32[6144]{0:T(1024)S(1)} %get-tuple-element.21), kind=kCustom, calls=%fused_computation.3 | custom fusion | bytes 6316032 | tf_op jit(solution)/shard_map/gather | solution.py:58
  357.6 21.1 %gather_fusion.2 = f32[6144,128]{1,0:T(8,128)} fusion(f32[384,128]{1,0:T(8,128)S(1)} %pad_maximum_fusion, s32[6144]{0:T(1024)S(1)} %get-tuple-element.20), kind=kCustom, calls=%fused_computation.2 | custom fusion | bytes 6316032 | tf_op jit(solution)/shard_map/gather | solution.py:58
  378.7 3.2 add.222
  381.8 3.0 fusion.9
  384.8 2.9 fusion.7
  388.1 4.9 %fusion.98 = f32[2048,512]{1,0:T(8,128)} fusion(f32[2048,128]{1,0:T(8,128)S(1)} %bitcast.105, f32[128,512]{1,0:T(8,128)S(1)} %copy-done.14), kind=kOutput, calls=%fused_computation.192 | convolution fusion | flops 1610612736 | bytes 5505024 | tf_op jit(solution)/shard_map/dot_general | solution.py:43
  393.1 46.9 %reduce-scatter.2.cloned.1.call-done = f32[2048,128]{1,0:T(8,128)} async-done(((f32[2048,512]{1,0:T(8,128)}), f32[2048,128]{1,0:T(8,128)}) %reduce-scatter.2.cloned.1.call-update) | async-done | bytes 1048592 | tf_op jit(solution)/shard_map/reduce_scatter | solution.py:157
  440.0 2.6 dynamic-slice_add_fusion
  (140 shorter events, 6.1 us)
Async XLA Ops:
  6.5 95.2 %copy-start = (f32[512,512]{1,0:T(8,128)S(1)}, f32[512,512]{1,0:T(8,128)}, u32[]{:S(2)}) copy-start(f32[512,512]{1,0:T(8,128)} %param.31) | copy-start | bytes 3145732
  14.3 14.2 %copy-start.5 = (f32[128,512]{1,0:T(8,128)S(1)}, f32[128,512]{1,0:T(8,128)}, u32[]{:S(2)}) copy-start(f32[128,512]{1,0:T(8,128)} %param.22) | copy-start | bytes 786436
  14.3 14.2 %copy-start.6 = (f32[512,128]{1,0:T(8,128)S(1)}, f32[512,128]{1,0:T(8,128)}, u32[]{:S(2)}) copy-start(f32[512,128]{1,0:T(8,128)} %param.24) | copy-start | bytes 786436
  28.9 14.2 %copy-start.3 = (f32[4096,128]{1,0:T(8,128)S(1)}, f32[4096,128]{1,0:T(8,128)}, u32[]{:S(2)}) copy-start(f32[4096,128]{1,0:T(8,128)} %gather_fusion) | copy-start | bytes 6291460
  43.1 3.8 copy-start.18
  43.1 5.8 %copy-start.7 = (f32[128,512]{1,0:T(8,128)S(1)}, f32[128,512]{1,0:T(8,128)}, u32[]{:S(2)}) copy-start(f32[128,512]{1,0:T(8,128)} %param.25) | copy-start | bytes 786436
  44.9 23.8 %copy-start.8 = (f32[512,128]{1,0:T(8,128)S(1)}, f32[512,128]{1,0:T(8,128)}, u32[]{:S(2)}) copy-start(f32[512,128]{1,0:T(8,128)} %param.28) | copy-start | bytes 786436
  44.9 23.8 %copy-start.16 = (f32[512]{0:T(512)S(1)}, f32[512]{0:T(512)}, u32[]{:S(2)}) copy-start(f32[512]{0:T(512)} %param.26) | copy-start | bytes 6148
  44.9 24.5 %copy-start.9 = (f32[512,128]{1,0:T(8,128)S(1)}, f32[512,128]{1,0:T(8,128)}, u32[]{:S(2)}) copy-start(f32[512,128]{1,0:T(8,128)} %param.29) | copy-start | bytes 786436
  75.7 25.2 %copy-start.17 = (s32[64,16]{0,1:T(8,128)S(1)}, s32[64,16]{0,1:T(8,128)}, u32[]{:S(2)}) copy-start(s32[64,16]{0,1:T(8,128)} %param.37) | copy-start | bytes 12292
  75.7 25.6 %copy-start.10 = (f32[512,128]{1,0:T(8,128)S(1)}, f32[512,128]{1,0:T(8,128)}, u32[]{:S(2)}) copy-start(f32[512,128]{1,0:T(8,128)} %param.27) | copy-start | bytes 786436
  75.7 26.8 %copy-start.4 = (f32[512,512]{1,0:T(8,128)S(1)}, f32[512,512]{1,0:T(8,128)}, u32[]{:S(2)}) copy-start(f32[512,512]{1,0:T(8,128)} %param.32) | copy-start | bytes 3145732
  75.7 207.5 %all-to-all-start.1 = ((f32[64,128,256]{1,2,0:T(8,128)}), f32[64,128,256]{1,2,0:T(8,128)}, u32[]{:S(2)}, u32[]{:S(2)}) async-start(f32[64,128,256]{1,2,0:T(8,128)} %copy_bitcast_fusion), calls=%async_computation.1 | async-start | bytes 16777216 | tf_op jit(solution)/shard_map/all_to_all | solution.py:14
  292.2 11.3 %copy-start.2 = (f32[64,128,256]{2,1,0:T(8,128)S(1)}, f32[64,128,256]{2,1,0:T(8,128)}, u32[]{:S(2)}) copy-start(f32[64,128,256]{2,1,0:T(8,128)} %copy.41) | copy-start | bytes 25165828
  299.9 11.6 %copy-start.11 = (f32[128,512]{1,0:T(8,128)S(1)}, f32[128,512]{1,0:T(8,128)}, u32[]{:S(2)}) copy-start(f32[128,512]{1,0:T(8,128)} %param.30) | copy-start | bytes 786436
  300.0 16.7 %copy-start.20 = (s32[48,2]{0,1:T(2,128)S(1)}, s32[48,2]{0,1:T(2,128)}, u32[]{:S(2)}) copy-start(s32[48,2]{0,1:T(2,128)} %param.40) | copy-start | bytes 1156
  300.0 16.8 %copy-start.15 = (s32[48,2,128]{2,1,0:T(2,128)S(1)}, s32[48,2,128]{2,1,0:T(2,128)}, u32[]{:S(2)}) copy-start(s32[48,2,128]{2,1,0:T(2,128)} %param.41) | copy-start | bytes 147460
  300.0 16.8 %copy-start.13 = (f32[512,128]{1,0:T(8,128)S(1)}, f32[512,128]{1,0:T(8,128)}, u32[]{:S(2)}) copy-start(f32[512,128]{1,0:T(8,128)} %param.34) | copy-start | bytes 786436
  303.5 24.2 %copy-start.12 = (f32[512,128]{1,0:T(8,128)S(1)}, f32[512,128]{1,0:T(8,128)}, u32[]{:S(2)}) copy-start(f32[512,128]{1,0:T(8,128)} %param.35) | copy-start | bytes 786436
  303.5 24.2 %copy-start.19 = (f32[512]{0:T(512)S(1)}, f32[512]{0:T(512)}, u32[]{:S(2)}) copy-start(f32[512]{0:T(512)} %param.33) | copy-start | bytes 6148
  313.1 14.2 %all-to-all-start.2 = ((f32[4,128,512]{2,1,0:T(8,128)}), f32[4,128,512]{2,1,0:T(8,128)S(1)}, u32[]{:S(2)}, u32[]{:S(2)}) async-start(f32[4,128,512]{2,1,0:T(8,128)} %broadcast_in_dim.21), calls=%async_computation.2 | async-start | bytes 2097152 | tf_op jit(solution)/shard_map/all_to_all | solution.py:19
  316.6 123.3 %reduce-scatter.2.cloned.1.call-start = ((), (), s32[]{:S(2)}) async-start(), calls=%async_computation.4 | async-start | bytes 5242880 | tf_op jit(solution)/shard_map/reduce_scatter | solution.py:157
  328.2 29.4 %collective-permute-start = (f32[128,128]{1,0:T(8,128)S(1)}, f32[128,128]{1,0:T(8,128)S(1)}, u32[]{:S(2)}, u32[]{:S(2)}) collective-permute-start(f32[128,128]{1,0:T(8,128)S(1)} %fusion.46), channel_id=1, source_target_pairs={{0,1},{1,2},{2,3},{3,4},{4,5},{5,6},{6,7},{7,8},{8,9},{9,10},{10,1... | collective-permute-start | bytes 196616 | tf_op jit(solution)/shard_map/ppermute | solution.py:36
  336.4 21.2 %collective-permute-start.1 = (f32[128,128]{1,0:T(8,128)S(1)}, f32[128,128]{1,0:T(8,128)S(1)}, u32[]{:S(2)}, u32[]{:S(2)}) collective-permute-start(f32[128,128]{1,0:T(8,128)S(1)} %fusion.46), channel_id=1, source_target_pairs={{1,0},{2,1},{3,2},{4,3},{5,4},{6,5},{7,6},{8,7},{9,8},{10,9},{11,1... | collective-permute-start | bytes 196616 | tf_op jit(solution)/shard_map/ppermute | solution.py:37
  381.8 6.3 %copy-start.14 = (f32[128,512]{1,0:T(8,128)S(1)}, f32[128,512]{1,0:T(8,128)}, u32[]{:S(2)}) copy-start(f32[128,512]{1,0:T(8,128)} %param.36) | copy-start | bytes 786436
  384.8 57.8 %copy-start.1 = (f32[512,512]{1,0:T(8,128)S(1)}, f32[512,512]{1,0:T(8,128)}, u32[]{:S(2)}) copy-start(f32[512,512]{1,0:T(8,128)} %param.31) | copy-start | bytes 3145732
Sparse Core Ops, SparseCore 0:
  393.2 46.7 reduce-scatter.1
